TPU v7x, 128 devices: a whole 4x4x4 slice. The times are simulated.
128 devices in a mesh: row: 8 (over y, x_hi), col: 16 (over x_lo, z, core).
Axes of the slice: x: 4 (x_hi: 2, x_lo: 2; x = x_hi * 2 + x_lo), y: 4, z: 4, core: 2. Of those that a mesh axis runs over, the one named last changes fastest.
Arguments:
- queries: bfloat16 [128, 512, 1536], P('row', 'col'), may hold values from -101 to 101
- fresh_keys: bfloat16 [128, 512, 1536], P('row', 'col'), may hold values from -7.2 to 7.2
- fresh_values: bfloat16 [128, 512, 1536], P('row', 'col'), may hold values from -16 to 16
- stale_keys: bfloat16 [128, 512, 1536], P('row', 'col'), may hold values from -7.1875 to 7.1875
- stale_values: bfloat16 [128, 512, 1536], P('row', 'col'), may hold values from -16 to 16
- weight_out: bfloat16 [1536, 3072], replicated, may hold values from -0.15625 to 0.15625
- gate: float32 [3072], replicated, may hold values from 0.5 to 4
- far_tiles: int32 [128, 80], replicated, may hold values from -1 to 127, as said below
- far_blocks: int32 [128, 80], replicated, may hold values from 0 to 63
- far_count: int32 [128], replicated, may hold values from 40 to 80, as said below
Outputs:
- branch_out: bfloat16 [128, 512, 3072], P('row', 'col')
Inputs may be any that keep to these rules, and one draw needn't show every extreme that they name: `far_tiles`: row t lists far_count[t] different tiles, none of them t and none of the tiles that touch t by a side or a corner; its other entries are -1. `far_blocks`: entries k >= far_count[t] of row t are not read. `far_count`: some tile reads exactly 80 far blocks.
All inputs are finite; a program needn't handle non-finite values.
Results may differ from a plain program's by a relative error of at most 0.0054.
Values may be sent and summed in bfloat16 or wider, within the bound.
A program may use at most 192 MiB of HBM per device.

v0:
```python
import jax
import jax.numpy as jnp
from jax import lax
from jax.sharding import PartitionSpec as P

HEADS = 12
HD = 128
R = 6
BLK = 8


def padded(value, sides, width):
    for axis, dim in sides:
        devices, length = (lax.axis_size(axis), value.shape[dim])
        up = [(i, (i + 1) % devices) for i in range(devices - 1)]
        down = [(j, i) for i, j in up]
        last = lax.slice_in_dim(value, length - width, length, axis=dim)
        leading = lax.slice_in_dim(value, 0, width, axis=dim)
        before = lax.ppermute(last, axis, up)
        after = lax.ppermute(leading, axis, down)
        value = jnp.concatenate([before, value, after], axis=dim)
    return value


def head_scores(query_rows, key_rows, allowed):
    query_heads = query_rows.reshape(query_rows.shape[0], HEADS, HD)
    key_heads = key_rows.reshape(key_rows.shape[0], HEADS, HD)
    products = jnp.einsum(
        "qhd,khd->hqk", query_heads, key_heads, preferred_element_type=jnp.float32
    )
    return jnp.where(allowed[None], products * HD ** (-0.5), -jnp.inf)


def weigh_values(weights, value_rows):
    value_heads = value_rows.reshape(value_rows.shape[0], HEADS, HD)
    return jnp.einsum(
        "hqk,khd->qhd",
        weights.astype(jnp.bfloat16),
        value_heads,
        preferred_element_type=jnp.float32,
    )


def window_mask(start_pos, query_count, key_span, radius, extent):
    query_pos = start_pos + jnp.arange(query_count, dtype=jnp.int32)
    key_pos = start_pos - radius + jnp.arange(key_span, dtype=jnp.int32)
    near_enough = jnp.abs(key_pos[None, :] - query_pos[:, None]) <= radius
    return near_enough & (key_pos[None, :] >= 0) & (key_pos[None, :] < extent)


def shards(
    queries,
    fresh_keys,
    fresh_values,
    stale_keys,
    stale_values,
    weight_out,
    gate,
    far_tiles,
    far_blocks,
    far_count,
):
    tile_rows, tile_cols, inner = queries.shape
    rows_axis = lax.axis_size("row")
    cols_axis = lax.axis_size("col")
    my_row = lax.axis_index("row")
    my_col = lax.axis_index("col")
    own_tile = my_row * cols_axis + my_col
    fresh_kv = jnp.concatenate([fresh_keys, fresh_values], axis=2)
    bordered = padded(fresh_kv, (("row", 0), ("col", 1)), R)
    stale_kv = jnp.concatenate([stale_keys, stale_values], axis=2).reshape(-1, BLK, 2 * inner)
    wanted = far_tiles == own_tile
    requested = jnp.any(wanted, axis=1)
    which_block = jnp.sum(jnp.where(wanted, far_blocks, 0), axis=1)
    outgoing = jnp.where(
        requested[:, None, None],
        jnp.take(stale_kv, which_block, axis=0),
        jnp.zeros((), stale_kv.dtype),
    )
    arrived = lax.all_to_all(outgoing, ("row", "col"), split_axis=0, concat_axis=0, tiled=True)
    own_list = lax.dynamic_index_in_dim(far_tiles, own_tile, 0, keepdims=False)
    own_count = lax.dynamic_index_in_dim(far_count, own_tile, 0, keepdims=False)
    is_live = jnp.arange(own_list.shape[0], dtype=jnp.int32) < own_count
    far_kv = jnp.take(arrived, jnp.where(is_live, own_list, 0), axis=0).reshape(-1, 2 * inner)
    far_live = jnp.repeat(is_live, BLK)
    far_mask = far_live[None, :]
    group_rows = 8
    col_mask = window_mask(
        my_col * tile_cols, tile_cols, tile_cols + 2 * R, R, cols_axis * tile_cols
    )
    pieces = []
    for start_row in range(0, tile_rows, group_rows):
        query_rows = queries[start_row : start_row + group_rows].reshape(-1, inner)
        near_kv = bordered[start_row : start_row + group_rows + 2 * R].reshape(-1, 2 * inner)
        row_mask = window_mask(
            my_row * tile_rows + start_row, group_rows, group_rows + 2 * R, R, rows_axis * tile_rows
        )
        near_mask = (row_mask[:, None, :, None] & col_mask[None, :, None, :]).reshape(
            group_rows * tile_cols, -1
        )
        near_scores = head_scores(query_rows, near_kv[:, :inner], near_mask)
        far_scores = head_scores(query_rows, far_kv[:, :inner], far_mask)
        peak = jnp.maximum(
            jnp.max(near_scores, axis=2, keepdims=True), jnp.max(far_scores, axis=2, keepdims=True)
        )
        near_weights = jnp.exp(near_scores - peak)
        far_weights = jnp.exp(far_scores - peak)
        denominator = jnp.sum(near_weights, axis=2) + jnp.sum(far_weights, axis=2)
        blended = weigh_values(near_weights, near_kv[:, inner:]) + weigh_values(
            far_weights, far_kv[:, inner:]
        )
        pieces.append((blended / denominator.T[:, :, None]).astype(jnp.bfloat16).reshape(-1, inner))
    attended = jnp.concatenate(pieces, axis=0)
    projected = jnp.dot(attended, weight_out, preferred_element_type=jnp.float32)
    return (projected * gate[None, :]).astype(jnp.bfloat16).reshape(tile_rows, tile_cols, -1)


def solution(mesh):
    return jax.shard_map(
        shards,
        mesh=mesh,
        in_specs=(
            P("row", "col", None),
            P("row", "col", None),
            P("row", "col", None),
            P("row", "col", None),
            P("row", "col", None),
            P(),
            P(),
            P(),
            P(),
            P(),
        ),
        out_specs=P("row", "col", None),
        check_vma=False,
    )
```

profile of v0, /device:TPU:26, one launch (start us, length us, event | category | flops | bytes accessed | tf_op | source)
XLA Modules:
  0.0 286.3 jit_solution(6519451601915525317)
XLA Ops:
  0.0 1.7 constant_dynamic-update-slice_fusion.1
  1.7 0.2 copy-done.9
  1.9 0.2 constant_dynamic-update-slice_fusion
  2.1 1.6 fusion.75
  3.7 4.0 %collective-permute-start = (bf16[6,32,3072]{2,1,0:T(8,128)(2,1)}, bf16[6,32,3072]{2,1,0:T(8,128)(2,1)}, u32[]{:S(2)}, u32[]{:S(2)}) collective-permute-start(bf16[6,32,3072]{2,1,0:T(8,128)(2,1)} %get-tuple-element.19), channel_id=1, source_target_pairs={{0,16},{16,32},{32,48},{48,64},{64,80},{80,96},{96,112},{1,17},{17... | collective-permute-start | bytes 3538952 | tf_op jit(solution)/shard_map/ppermute | solution.py:19
  7.7 4.2 %collective-permute-start.1 = (bf16[6,32,3072]{2,1,0:T(8,128)(2,1)}, bf16[6,32,3072]{2,1,0:T(8,128)(2,1)}, u32[]{:S(2)}, u32[]{:S(2)}) collective-permute-start(bf16[6,32,3072]{2,1,0:T(8,128)(2,1)} %get-tuple-element.20), channel_id=1, source_target_pairs={{16,0},{32,16},{48,32},{64,48},{80,64},{96,80},{112,96},{17,1},{33... | collective-permute-start | bytes 3538952 | tf_op jit(solution)/shard_map/ppermute | solution.py:20
  12.0 3.9 %pad_maximum_fusion.1 = bf16[16,32,3072]{2,1,0:T(8,128)(2,1)} fusion(bf16[16,32,1536]{2,1,0:T(8,128)(2,1)} %param.14, bf16[16,32,1536]{2,1,0:T(8,128)(2,1)} %param.13), kind=kLoop, calls=%fused_computation.48 | loop fusion | flops 6291456 | bytes 6291456 | tf_op jit(solution)/shard_map/concatenate | solution.py:71
  15.9 5.5 %gather_fusion = bf16[128,8,3072]{2,1,0:T(8,128)(2,1)} fusion(bf16[64,8,3072]{2,1,0:T(8,128)(2,1)} %bitcast.90, s32[1024]{0:T(1024)S(1)} %pad_clamp_fusion.1), kind=kCustom, calls=%fused_computation | custom fusion | bytes 12583424 | tf_op jit(solution)/shard_map/jit(_take)/gather | solution.py:77
  21.4 7.0 %select_select_fusion = bf16[128,8,3072]{2,1,0:T(8,128)(2,1)} fusion(bf16[128,8,3072]{2,1,0:T(8,128)(2,1)} %gather_fusion, pred[128]{0:T(512)(128)(4,1)S(1)} %compare_and_fusion, pred[128]{0:T(512)(128)(4,1)S(1)} %get-tuple-element.7), kind=kLoop, calls=%fused_computation.22 | loop fusion | flops 6291456 | bytes 12583168 | tf_op jit(solution)/shard_map/jit(_where)/select_n | solution.py:75
  28.4 10.6 %all-to-all-start = ((bf16[128,8,3072]{2,1,0:T(8,128)(2,1)}), bf16[128,8,3072]{2,1,0:T(8,128)(2,1)}, u32[]{:S(2)}, u32[]{:S(2)}) async-start(bf16[128,8,3072]{2,1,0:T(8,128)(2,1)} %select_select_fusion), calls=%async_computation | async-start | bytes 12582912 | tf_op jit(solution)/shard_map/all_to_all | solution.py:80
  39.1 0.7 dynamic_slice.8
  39.9 0.1 fusion.54
  40.0 2.1 broadcast_and_fusion.1
  42.1 0.7 iota_compare_fusion
  42.8 0.1 broadcast_in_dim.112
  43.0 0.2 dynamic-slice_reduce_fusion
  43.1 21.4 %collective-permute-done.1 = bf16[6,32,3072]{2,1,0:T(8,128)(2,1)} collective-permute-done((bf16[6,32,3072]{2,1,0:T(8,128)(2,1)}, bf16[6,32,3072]{2,1,0:T(8,128)(2,1)}, u32[]{:S(2)}, u32[]{:S(2)}) %collective-permute-start.1) | collective-permute-done | bytes 1179680 | tf_op jit(solution)/shard_map/ppermute | solution.py:20
  64.5 1.7 pad_maximum_fusion.4
  66.2 1.6 copy.76
  67.8 1.6 copy.77
  69.4 15.1 %collective-permute-start.3 = (bf16[28,6,3072]{2,0,1:T(8,128)(2,1)}, bf16[28,6,3072]{2,0,1:T(8,128)(2,1)}, u32[]{:S(2)}, u32[]{:S(2)}) collective-permute-start(bf16[28,6,3072]{2,0,1:T(8,128)(2,1)} %copy.77), channel_id=1, source_target_pairs={{1,0},{2,1},{3,2},{4,3},{5,4},{6,5},{7,6},{8,7},{9,8},{10,9},{11,1... | collective-permute-start | bytes 3096584 | tf_op jit(solution)/shard_map/ppermute | solution.py:20
  84.5 2.2 collective-permute-start.2
  86.7 0.7 compare_and_fusion.1
  87.5 0.1 broadcast_in_dim.116
  87.6 2.1 and.137
  89.7 1.0 copy.81
  90.7 2.8 and.146
  93.5 1.3 copy.92
  94.8 2.6 fusion.76
  97.5 2.4 reshape_reshape.8
  99.8 2.4 reshape_reshape.9
  102.2 0.7 fusion.60
  102.9 42.2 %collective-permute-done.3 = bf16[28,6,3072]{2,0,1:T(8,128)(2,1)} collective-permute-done((bf16[28,6,3072]{2,0,1:T(8,128)(2,1)}, bf16[28,6,3072]{2,0,1:T(8,128)(2,1)}, u32[]{:S(2)}, u32[]{:S(2)}) %collective-permute-start.3) | collective-permute-done | bytes 1032224 | tf_op jit(solution)/shard_map/ppermute | solution.py:20
  145.2 1.9 copy.79
  147.0 14.4 %collective-permute-done.2 = bf16[28,6,3072]{2,0,1:T(8,128)(2,1)} collective-permute-done((bf16[28,6,3072]{2,0,1:T(8,128)(2,1)}, bf16[28,6,3072]{2,0,1:T(8,128)(2,1)}, u32[]{:S(2)}, u32[]{:S(2)}) %collective-permute-start.2) | collective-permute-done | bytes 1032224 | tf_op jit(solution)/shard_map/ppermute | solution.py:19
  161.4 1.9 copy.78
  163.3 5.8 %pad_maximum_fusion = bf16[28,44,3072]{2,1,0:T(8,128)(2,1)S(1)} fusion(bf16[28,6,3072]{2,1,0:T(8,128)(2,1)S(1)} %copy.79, bf16[6,32,3072]{2,1,0:T(8,128)(2,1)} %collective-permute-done.1, bf16[16,32,3072]{2,1,0:T(8,128)(2,1)S(1)} %constant_dynamic-update-slice_fusion, bf16[6,32,3072]{2,1,0:T(8,128)(2,1)} %collective-permute-done, ...), kind=kLoop, calls=%fused_computation.10 | loop fusion | flops 37847040 | bytes 15138816 | tf_op jit(solution)/shard_map/concatenate | solution.py:21
  169.1 4.6 %fusion.71 = (bf16[20,44,3072]{2,1,0:T(8,128)(2,1)}, bf16[20,44,3072]{2,1,0:T(8,128)(2,1)}) fusion(bf16[28,44,3072]{2,1,0:T(8,128)(2,1)S(1)} %pad_maximum_fusion), kind=kLoop, calls=%fused_computation.119 | loop fusion | bytes 21626880 | tf_op jit(solution)/shard_map/slice | solution.py:94
  173.7 8.5 %reshape.347 = bf16[880,3072]{1,0:T(8,128)(2,1)} reshape(bf16[20,44,3072]{2,1,0:T(8,128)(2,1)} %get-tuple-element.9) | data formatting | bytes 10813440 | tf_op jit(solution)/shard_map/reshape | solution.py:94
  182.2 4.4 %fusion.72 = (bf16[880,1536]{1,0:T(8,128)(2,1)S(1)}, bf16[880,1536]{1,0:T(8,128)(2,1)}) fusion(bf16[880,3072]{1,0:T(8,128)(2,1)} %reshape.347), kind=kLoop, calls=%fused_computation.120 | loop fusion | bytes 10813440 | tf_op jit(solution)/shard_map/slice | solution.py:109
  186.6 2.8 copy.80
  189.4 3.3 %copy.82 = bf16[880,1536]{0,1:T(8,128)(2,1)S(1)} copy(bf16[880,1536]{1,0:T(8,128)(2,1)} %get-tuple-element.14) | data formatting | bytes 5406720 | tf_op jit(solution)/shard_map/slice | solution.py:101
  192.7 8.5 %reshape.354 = bf16[880,3072]{1,0:T(8,128)(2,1)} reshape(bf16[20,44,3072]{2,1,0:T(8,128)(2,1)} %get-tuple-element.10) | data formatting | bytes 10813440 | tf_op jit(solution)/shard_map/reshape | solution.py:94
  201.1 5.4 %fusion.73 = (bf16[880,1536]{1,0:T(8,128)(2,1)}, bf16[880,1536]{1,0:T(8,128)(2,1)}) fusion(bf16[880,3072]{1,0:T(8,128)(2,1)} %reshape.354), kind=kLoop, calls=%fused_computation.121 | loop fusion | bytes 10813440 | tf_op jit(solution)/shard_map/slice | solution.py:101
  206.5 4.5 %copy.93 = bf16[880,1536]{0,1:T(8,128)(2,1)} copy(bf16[880,1536]{1,0:T(8,128)(2,1)} %get-tuple-element.15) | data formatting | bytes 5406720 | tf_op jit(solution)/shard_map/slice | solution.py:101
  211.0 5.0 %copy.91 = bf16[880,1536]{0,1:T(8,128)(2,1)} copy(bf16[880,1536]{1,0:T(8,128)(2,1)} %get-tuple-element.16) | data formatting | bytes 5406720 | tf_op jit(solution)/shard_map/slice | solution.py:109
  216.1 7.4 %fusion.4 = (f32[12,256]{1,0:T(8,128)S(1)}, f32[12,880,256]{2,1,0:T(8,128)}) fusion(pred[256,880]{0,1:T(8,128)(4,1)S(1)} %copy-done.6, bf16[880,12,128]{0,2,1:T(8,128)(2,1)S(1)} %bitcast.91, bf16[256,12,128]{2,1,0:T(8,128)(2,1)} %reshape_reshape.8), kind=kOutput, calls=%fused_computation.11 | convolution fusion | flops 700167168 | bytes 14540800 | tf_op jit(solution)/shard_map/qhd,khd->hqk/dot_general | solution.py:28
  223.5 6.3 %fusion.5 = (f32[12,256]{1,0:T(8,128)S(1)}, f32[12,880,256]{2,1,0:T(8,128)}) fusion(pred[256,880]{0,1:T(8,128)(4,1)S(1)} %copy.92, bf16[880,12,128]{0,2,1:T(8,128)(2,1)S(1)} %bitcast.92, bf16[256,12,128]{2,1,0:T(8,128)(2,1)S(1)} %copy-done.3), kind=kOutput, calls=%fused_computation.12 | convolution fusion | flops 700167168 | bytes 14540800 | tf_op jit(solution)/shard_map/qhd,khd->hqk/dot_general | solution.py:28
  229.8 5.8 %gather_fusion.1 = bf16[80,8,3072]{2,1,0:T(8,128)(2,1)} fusion(bf16[128,8,3072]{2,1,0:T(8,128)(2,1)} %all-to-all-done, s32[1024]{0:T(1024)S(1)} %pad_clamp_fusion), kind=kCustom, calls=%fused_computation.1 | custom fusion | bytes 7864640 | tf_op jit(solution)/shard_map/jit(_take)/gather | solution.py:84
  235.6 2.5 bitcast_select_fusion.2
  238.2 1.7 fusion.74
  239.8 2.3 copy.89
  242.1 2.9 %copy.85 = bf16[640,1536]{0,1:T(8,128)(2,1)S(1)} copy(bf16[640,1536]{1,0:T(8,128)(2,1)} %get-tuple-element.18) | data formatting | bytes 3932160 | tf_op jit(solution)/shard_map/slice | solution.py:102
  245.1 2.0 bitcast_reduce_fusion.1
  247.1 6.8 %fusion = f32[12,256]{1,0:T(8,128)S(1)} fusion(f32[12,880,256]{2,1,0:T(8,128)} %get-tuple-element.28, f32[12,256]{1,0:T(8,128)S(1)} %max.16, pred[256,880]{0,1:T(8,128)(4,1)S(1)} %copy-done.7), kind=kLoop, calls=%fused_computation.6 | loop fusion | flops 10810368 | bytes 11063296 | tf_op jit(solution)/shard_map/reduce_sum | solution.py:108
  253.9 5.9 %fusion.14 = f32[12,128,256]{2,1,0:T(8,128)} fusion(bf16[880,12,128]{0,2,1:T(8,128)(2,1)} %bitcast.96, f32[12,880,256]{2,1,0:T(8,128)S(1)} %bitcast.89, f32[12,256]{1,0:T(8,128)S(1)} %max.16, pred[256,880]{0,1:T(8,128)(4,1)S(1)} %copy-done.7), kind=kOutput, calls=%fused_computation.28 | convolution fusion | flops 702873600 | bytes 15327232 | tf_op jit(solution)/shard_map/hqk,khd->qhd/dot_general | solution.py:36
  259.8 5.9 %fusion.8 = (f32[12,256]{1,0:T(8,128)S(1)}, f32[12,256]{1,0:T(8,128)S(1)}, f32[12,640,256]{2,1,0:T(8,128)}) fusion(f32[12,640,256]{2,1,0:T(8,128)S(1)} %get-tuple-element.30, f32[12,256]{1,0:T(8,128)S(1)} %max.16, pred[640]{0:T(1024)(128)(4,1)S(1)} %broadcast_in_dim.112, bf16[640,12,128]{0,2,1:T(8,128)(2,1)S(1)} %bitcast.94, ...), kind=kOutput, calls=%fused_computation.23 | convolution fusion | flops 517072896 | bytes 18518656 | tf_op jit(solution)/shard_map/qhd,khd->hqk/dot_general | solution.py:28
  265.8 1.0 slice-done.2
  266.8 2.2 fusion.2
  269.0 3.9 %fusion.12 = f32[12,128,256]{2,1,0:T(8,128)} fusion(bf16[880,12,128]{0,2,1:T(8,128)(2,1)S(1)} %bitcast.95, f32[12,880,256]{2,1,0:T(8,128)S(1)} %bitcast.87, f32[12,256]{1,0:T(8,128)S(1)} %max.17, pred[256,880]{0,1:T(8,128)(4,1)S(1)} %copy.92), kind=kOutput, calls=%fused_computation.27 | convolution fusion | flops 702873600 | bytes 15327232 | tf_op jit(solution)/shard_map/hqk,khd->qhd/dot_general | solution.py:36
  273.0 1.9 fusion.10
  275.0 2.2 fusion.40
  277.2 2.2 fusion.39
  279.5 6.6 %multiply_convert_fusion = bf16[512,3072]{1,0:T(8,128)(2,1)} fusion(bf16[1536,3072]{1,0:T(8,128)(2,1)S(1)} %bitcast.100, f32[3072]{0:T(1024)S(1)} %copy-done.12, bf16[256,1536]{0,1:T(8,128)(2,1)S(1)} %bitcast.102, bf16[256,1536]{0,1:T(8,128)(2,1)S(1)} %bitcast.101), kind=kOutput, calls=%fused_computation.21 | convolution fusion | flops 4838129664 | bytes 14168064 | tf_op jit(solution)/shard_map/dot_general | solution.py:114
  (76 shorter events, 0.6 us)
Async XLA Ops:
  0.0 1.9 copy-start.9
  1.9 10.1 %copy-start.10 = (s32[128,80]{0,1:T(8,128)S(1)}, s32[128,80]{0,1:T(8,128)}, u32[]{:S(2)}) copy-start(s32[128,80]{0,1:T(8,128)} %param.17) | copy-start | bytes 122884
  1.9 10.1 %copy-start.11 = (s32[128,80]{0,1:T(8,128)S(1)}, s32[128,80]{0,1:T(8,128)}, u32[]{:S(2)}) copy-start(s32[128,80]{0,1:T(8,128)} %param.18) | copy-start | bytes 122884
  3.7 39.5 %collective-permute-start = (bf16[6,32,3072]{2,1,0:T(8,128)(2,1)}, bf16[6,32,3072]{2,1,0:T(8,128)(2,1)}, u32[]{:S(2)}, u32[]{:S(2)}) collective-permute-start(bf16[6,32,3072]{2,1,0:T(8,128)(2,1)} %get-tuple-element.19), channel_id=1, source_target_pairs={{0,16},{16,32},{32,48},{48,64},{64,80},{80,96},{96,112},{1,17},{17... | collective-permute-start | bytes 3538952 | tf_op jit(solution)/shard_map/ppermute | solution.py:19
  7.7 56.8 %collective-permute-start.1 = (bf16[6,32,3072]{2,1,0:T(8,128)(2,1)}, bf16[6,32,3072]{2,1,0:T(8,128)(2,1)}, u32[]{:S(2)}, u32[]{:S(2)}) collective-permute-start(bf16[6,32,3072]{2,1,0:T(8,128)(2,1)} %get-tuple-element.20), channel_id=1, source_target_pairs={{16,0},{32,16},{48,32},{64,48},{80,64},{96,80},{112,96},{17,1},{33... | collective-permute-start | bytes 3538952 | tf_op jit(solution)/shard_map/ppermute | solution.py:20
  28.4 10.7 %copy-start.13 = (s32[128]{0:T(128)S(1)}, s32[128]{0:T(128)}, u32[]{:S(2)}) copy-start(s32[128]{0:T(128)} %param.19) | copy-start | bytes 1540
  28.4 201.5 %all-to-all-start = ((bf16[128,8,3072]{2,1,0:T(8,128)(2,1)}), bf16[128,8,3072]{2,1,0:T(8,128)(2,1)}, u32[]{:S(2)}, u32[]{:S(2)}) async-start(bf16[128,8,3072]{2,1,0:T(8,128)(2,1)} %select_select_fusion), calls=%async_computation | async-start | bytes 12582912 | tf_op jit(solution)/shard_map/all_to_all | solution.py:80
  69.4 75.8 %collective-permute-start.3 = (bf16[28,6,3072]{2,0,1:T(8,128)(2,1)}, bf16[28,6,3072]{2,0,1:T(8,128)(2,1)}, u32[]{:S(2)}, u32[]{:S(2)}) collective-permute-start(bf16[28,6,3072]{2,0,1:T(8,128)(2,1)} %copy.77), channel_id=1, source_target_pairs={{1,0},{2,1},{3,2},{4,3},{5,4},{6,5},{7,6},{8,7},{9,8},{10,9},{11,1... | collective-permute-start | bytes 3096584 | tf_op jit(solution)/shard_map/ppermute | solution.py:20
  84.5 76.9 %collective-permute-start.2 = (bf16[28,6,3072]{2,0,1:T(8,128)(2,1)}, bf16[28,6,3072]{2,0,1:T(8,128)(2,1)}, u32[]{:S(2)}, u32[]{:S(2)}) collective-permute-start(bf16[28,6,3072]{2,0,1:T(8,128)(2,1)} %copy.76), channel_id=1, source_target_pairs={{0,1},{1,2},{2,3},{3,4},{4,5},{5,6},{6,7},{7,8},{8,9},{9,10},{10,1... | collective-permute-start | bytes 3096584 | tf_op jit(solution)/shard_map/ppermute | solution.py:19
  211.0 5.0 %copy-start.6 = (pred[256,880]{0,1:T(8,128)(4,1)S(1)}, pred[256,880]{0,1:T(8,128)(4,1)}, u32[]{:S(2)}) copy-start(pred[256,880]{0,1:T(8,128)(4,1)} %copy.81) | copy-start | bytes 675844
  216.1 7.5 %copy-start = (bf16[880,1536]{0,1:T(8,128)(2,1)S(1)}, bf16[880,1536]{0,1:T(8,128)(2,1)}, u32[]{:S(2)}) copy-start(bf16[880,1536]{0,1:T(8,128)(2,1)} %copy.93) | copy-start | bytes 8110084
  216.1 7.5 %copy-start.3 = (bf16[256,12,128]{2,1,0:T(8,128)(2,1)S(1)}, bf16[256,12,128]{2,1,0:T(8,128)(2,1)}, u32[]{:S(2)}) copy-start(bf16[256,12,128]{2,1,0:T(8,128)(2,1)} %reshape_reshape.9) | copy-start | bytes 2359300
  239.8 5.2 %copy-start.2 = (bf16[256,12,128]{2,1,0:T(8,128)(2,1)S(1)}, bf16[256,12,128]{2,1,0:T(8,128)(2,1)}, u32[]{:S(2)}) copy-start(bf16[256,12,128]{2,1,0:T(8,128)(2,1)} %reshape_reshape.8) | copy-start | bytes 2359300
  245.1 2.0 copy-start.7
  245.1 8.8 %slice-start.3 = ((s8[10813440]{0:T(1024)(128)(4,1)}), s8[4194304]{0:T(1024)(128)(4,1)S(1)}, s32[]{:S(2)}) async-start(s8[10813440]{0:T(1024)(128)(4,1)} %bitcast.88), calls=%async_computation.4 | async-start | bytes 8388608
  245.1 8.8 %slice-start.4 = ((s8[10813440]{0:T(1024)(128)(4,1)}), s8[4194304]{0:T(1024)(128)(4,1)S(1)}, s32[]{:S(2)}) async-start(s8[10813440]{0:T(1024)(128)(4,1)} %bitcast.88), calls=%async_computation.5 | async-start | bytes 8388608
  247.1 6.8 %slice-start.5 = ((s8[10813440]{0:T(1024)(128)(4,1)}), s8[2424832]{0:T(1024)(128)(4,1)S(1)}, s32[]{:S(2)}) async-start(s8[10813440]{0:T(1024)(128)(4,1)} %bitcast.88), calls=%async_computation.6 | async-start | bytes 4849664
  253.9 5.9 %copy-start.4 = (bf16[256,12,128]{2,1,0:T(8,128)(2,1)S(1)}, bf16[256,12,128]{2,1,0:T(8,128)(2,1)}, u32[]{:S(2)}) copy-start(bf16[256,12,128]{2,1,0:T(8,128)(2,1)} %reshape_reshape.9) | copy-start | bytes 2359300
  259.8 6.0 %slice-start = ((s8[10813440]{0:T(1024)(128)(4,1)}), s8[4194304]{0:T(1024)(128)(4,1)S(1)}, s32[]{:S(2)}) async-start(s8[10813440]{0:T(1024)(128)(4,1)} %bitcast.86), calls=%async_computation.1 | async-start | bytes 8388608
  259.8 6.0 %slice-start.1 = ((s8[10813440]{0:T(1024)(128)(4,1)}), s8[4194304]{0:T(1024)(128)(4,1)S(1)}, s32[]{:S(2)}) async-start(s8[10813440]{0:T(1024)(128)(4,1)} %bitcast.86), calls=%async_computation.2 | async-start | bytes 8388608
  259.8 7.0 %slice-start.2 = ((s8[10813440]{0:T(1024)(128)(4,1)}), s8[2424832]{0:T(1024)(128)(4,1)S(1)}, s32[]{:S(2)}) async-start(s8[10813440]{0:T(1024)(128)(4,1)} %bitcast.86), calls=%async_computation.3 | async-start | bytes 4849664
  266.8 2.2 copy-start.5
  269.0 4.0 %copy-start.1 = (f32[12,640,256]{2,1,0:T(8,128)S(1)}, f32[12,640,256]{2,1,0:T(8,128)}, u32[]{:S(2)}) copy-start(f32[12,640,256]{2,1,0:T(8,128)} %get-tuple-element.31) | copy-start | bytes 23592964
  273.0 2.0 copy-start.8
  273.0 2.0 copy-start.14
  275.0 2.2 copy-start.15
  275.0 4.4 %slice-start.6 = ((s8[9437184]{0:T(1024)(128)(4,1)}), s8[4194304]{0:T(1024)(128)(4,1)S(1)}, s32[]{:S(2)}) async-start(s8[9437184]{0:T(1024)(128)(4,1)} %bitcast.99), calls=%async_computation.7 | async-start | bytes 8388608
  275.0 4.4 %slice-start.7 = ((s8[9437184]{0:T(1024)(128)(4,1)}), s8[4194304]{0:T(1024)(128)(4,1)S(1)}, s32[]{:S(2)}) async-start(s8[9437184]{0:T(1024)(128)(4,1)} %bitcast.99), calls=%async_computation.8 | async-start | bytes 8388608
  277.2 2.2 slice-start.8
  277.2 2.2 copy-start.12
where the time goes:
time: 292 us; the launch traced here: 286 us
  local copies, waits for them, and re-layouts  92.7 us (32%)
  waiting for transfers between devices  78 us (27%)
  matrix products  42.4 us (15%)
  other arithmetic  36.3 us (12%)
  starting transfers between devices  36.1 us (12%)
    ppermute x2, waiting for transfers between devices, padded(): after = lax.ppermute(leading, axis, down)  63.6 us
    dot_general x4, matrix products, head_scores(): jnp.einsum('qhd,khd->hqk', query_heads, key_heads, preferred_element_type...  21.6 us
    ppermute x2, starting transfers between devices, padded(): after = lax.ppermute(leading, axis, down)  19.3 us
    reshape x2, local copies, waits for them, and re-layouts, shards(): bordered[start_row:start_row + group_rows + 2 * R].reshape(-1, 2 * inner)  16.9 us
    ppermute x2, waiting for transfers between devices, padded(): before = lax.ppermute(last, axis, up)  14.4 us
    dot_general x4, matrix products, weigh_values(): jnp.einsum('hqk,khd->qhd', weights.astype(jnp.bfloat16), value_heads, pre...  14.2 us
    slice x3, local copies, waits for them, and re-layouts, shards(): near_scores = head_scores(query_rows, near_kv[:, :inner], near_mask)  13.2 us
    slice x3, local copies, waits for them, and re-layouts, shards(): near_kv[:, inner:]  12.2 us
  transfers between devices with their start and end apart: 5, of which 3 were waited for; matrix products, arithmetic and copies ran while one was open for 39% of the time, Pallas kernels for 0%

commit v1 on v0

v1 whole, which is shorter than its diff:
```python
import jax
import jax.numpy as jnp
from jax import lax
from jax.experimental import pallas as pl
from jax.experimental.pallas import tpu as pltpu
from jax.sharding import PartitionSpec as P

HD = 128
R = 6
BLK = 8
ROWS = 8
COLS = 16
TH = 16
TW = 32
HALF = 256
LOW = -1e30
SCALE = HD ** (-0.5) * 1.4426950408889634
MESH = pl.DeviceIdType.MESH

CLOSE = 29
EDGE = [(i, f, e) for i in (-1, 0, 1) for f in (0, 1) for e in (-1, 1)] + [(-1, 0, 0), (1, 0, 0)]
UNUSED = CLOSE + len(EDGE)
MAIN = UNUSED + 1
MIX = 25
SLOTS = 128
N_MAIN = SLOTS - MAIN
MID = COLS // 2
GROUPS = ((0, 48), (48, 32), (80, 32), (112, 16))
EARLY, LATE = 3, 4


def blend(late, before, after):
    return before + late * (after - before)


def close_offset(j):
    dr = blend(j // 24, 2 + 2 * (j % 3), 0)
    e = blend(j // 24, j // 3, j - 22)
    return dr, 0, e


def edge_offset(i):
    last = i // 12
    return blend(last, i // 4 - 1, 2 * (i - 12) - 1), blend(last, i // 2 % 2, 0), blend(last, 2 * (i % 2) - 1, 0)


def main_offset(p):
    i = MIX * p % N_MAIN
    straight = i // 58
    k = i - 40
    e1 = blend(i // 40, i // 5, k // 3 + (k // 3 + 5) // 6)
    dr1 = blend(i // 40, 2 + i % 5, 7 + k % 3)
    k = i - 58
    e2 = blend(i // 74, k // 2, 2 + (k - 16) // 2)
    dr2 = blend(i // 74, 3 + 2 * (k % 2), 7 + 2 * (k % 2))
    return blend(straight, dr1, dr2), 1 - straight, blend(straight, e1, e2)


def tile_at(row, col, dr, f, e):
    return (row + dr + 2 * ROWS) % ROWS, (col // MID + f + 2) % 2 * MID + (col % MID + e + 2 * MID) % MID


ROW_AT, COL_AT, PAD_AT, DEAD_AT = 0, TH + 2 * R, TH + TW + 4 * R, TH + TW + 4 * R + 1

NORTH, SOUTH, WEST, EAST, NW, NE, SW, SE = range(8)
BAND = R * TW
CORNER = 48
SIDE = TH * R
STRIP = SIDE + 2 * CORNER
OWN_SPAN = (TH - 2) * TW


def kernel(
    q_hbm, k_hbm, v_hbm, sk_hbm, sv_hbm, far_lists, block_of, att_hbm,
    q_ref, k_ref, v_ref, sk_ref, sv_ref,
    kn_ref, ks_ref, kw_ref, ke_ref, vn_ref, vs_ref, vw_ref, ve_ref,
    pack_ref, side_ref, corner_ref,
    far_ref, stage_ref, acc_ref, m_ref, l_ref, query_marks, own_marks, north_marks, south_marks, west_marks, east_marks, far_marks,
    live_ref, att_ref,
    load_sem, halo_send, halo_recv, far_send, far_recv, edge_send, edge_recv, out_sem,
):
    heads = q_ref.shape[1] // HD
    row = lax.axis_index("row")
    col = lax.axis_index("col")
    has_n, has_s = row > 0, row < ROWS - 1
    has_w, has_e = col > 0, col < COLS - 1
    exists = {
        NORTH: has_n, SOUTH: has_s, WEST: has_w, EAST: has_e,
        NW: has_n & has_w, NE: has_n & has_e, SW: has_s & has_w, SE: has_s & has_e,
    }

    crossing = {NW: col == MID - 1, SW: col == MID - 1, NE: col == MID, SE: col == MID}

    def halo_copies(piece, straight=False):
        up, down = (row - 1 + ROWS) % ROWS, (row + 1) % ROWS
        left, right = (col - 1 + COLS) % COLS, (col + 1) % COLS
        lower, upper = pl.ds(TH - R, R), pl.ds(0, R)
        top, middle, bottom = pl.ds(0, CORNER), pl.ds(CORNER, SIDE), pl.ds(CORNER + SIDE, CORNER)
        plan = {
            NORTH: (has_s, (down, col), (k_hbm.at[lower], v_hbm.at[lower]), (kn_ref, vn_ref)),
            SOUTH: (has_n, (up, col), (k_hbm.at[upper], v_hbm.at[upper]), (ks_ref, vs_ref)),
            WEST: (has_e, (row, right), (side_ref.at[0], side_ref.at[1]), (kw_ref.at[middle], vw_ref.at[middle])),
            EAST: (has_w, (row, left), (side_ref.at[2], side_ref.at[3]), (ke_ref.at[middle], ve_ref.at[middle])),
            NW: (has_n & has_e, (row, right), (corner_ref.at[0], corner_ref.at[1]), (kw_ref.at[top], vw_ref.at[top])),
            NE: (has_n & has_w, (row, left), (corner_ref.at[2], corner_ref.at[3]), (ke_ref.at[top], ve_ref.at[top])),
            SW: (has_s & has_e, (row, right), (corner_ref.at[4], corner_ref.at[5]),
                 (kw_ref.at[bottom], vw_ref.at[bottom])),
            SE: (has_s & has_w, (row, left), (corner_ref.at[6], corner_ref.at[7]),
                 (ke_ref.at[bottom], ve_ref.at[bottom])),
        }
        sends, target, srcs, dsts = plan[piece]
        if piece in crossing:
            if straight:
                sends = crossing[piece] & (has_s if piece in (NW, NE) else has_n)
                target = (down if piece in (NW, NE) else up, target[1])
            else:
                sends = sends & jnp.logical_not(crossing[piece])
        copies = [
            pltpu.make_async_remote_copy(
                src_ref=src, dst_ref=dst,
                send_sem=halo_send.at[2 * piece + i], recv_sem=halo_recv.at[2 * piece + i],
                device_id=target, device_id_type=MESH,
            )
            for i, (src, dst) in enumerate(zip(srcs, dsts))
        ]
        return sends, copies

    def start_halo(piece, straight=False):
        sends, copies = halo_copies(piece, straight)

        @pl.when(sends)
        def _():
            for copy in copies:
                copy.start()

    def wait_halo(piece):
        _, copies = halo_copies(piece)

        @pl.when(exists[piece])
        def _():
            for copy in copies:
                copy.wait_recv()

    def wait_halo_sent(piece, straight=False):
        sends, copies = halo_copies(piece, straight)

        @pl.when(sends)
        def _():
            for copy in copies:
                copy.wait_send()

    start_halo(NORTH)
    start_halo(SOUTH)

    loads = [
        pltpu.make_async_copy(src, dst, load_sem.at[i])
        for i, (src, dst) in enumerate(
            ((sk_hbm, sk_ref), (sv_hbm, sv_ref), (k_hbm, k_ref), (v_hbm, v_ref), (q_hbm, q_ref))
        )
    ]
    for load in loads:
        load.start()

    def far_copy(slot, target, send_sem, recv_sem):
        return pltpu.make_async_remote_copy(
            src_ref=stage_ref.at[slot], dst_ref=far_ref.at[slot], send_sem=send_sem, recv_sem=recv_sem,
            device_id=target, device_id_type=MESH,
        )

    def fill(slot, target):
        block = block_of[target[0] * COLS + target[1]]
        pair, odd = lax.shift_right_logical(block, 1), block & 1
        both = []
        for ref in (sk_ref, sv_ref):
            rows = ref[pair].astype(jnp.float32)
            both.append(jnp.where(odd == 1, rows[BLK:], rows[:BLK]))
        stage_ref[slot] = jnp.concatenate(both, axis=0).astype(jnp.bfloat16)

    def send_far(slot, offset, sem):
        target = tile_at(row, col, *offset)
        fill(slot, target)
        far_copy(slot, target, far_send, far_recv.at[sem]).start()

    loads[0].wait()
    loads[1].wait()

    @pl.loop(0, CLOSE)
    def _(j):
        send_far(j, close_offset(j), 0)

    def send_main(p):
        send_far(MAIN + p, main_offset(p), (MAIN + p - 16) // 32)

    def touches(dr, other):
        return (row + dr >= 0) & (row + dr < ROWS) & (other[1] - col >= -1) & (other[1] - col <= 1)

    def edge(i):
        dr, f, e = EDGE[i]
        target, origin = tile_at(row, col, dr, f, e), tile_at(row, col, -dr, -f, -e)
        copy = far_copy(CLOSE + i, target, edge_send.at[i], edge_recv.at[i])
        return target, jnp.logical_not(touches(dr, target)), jnp.logical_not(touches(-dr, origin)), copy

    for i in range(len(EDGE)):
        target, sends, receives, copy = edge(i)

        @pl.when(sends)
        def _(i=i, target=target, copy=copy):
            fill(CLOSE + i, target)
            copy.start()

        @pl.when(jnp.logical_not(receives))
        def _(i=i):
            far_ref[CLOSE + i] = jnp.zeros(far_ref.shape[1:], far_ref.dtype)

    far_ref[UNUSED] = jnp.zeros(far_ref.shape[1:], far_ref.dtype)

    def pack(source, first, count, right, target):
        for r in range(count):
            if right:
                edge = source[first + r, TW - 16:].astype(jnp.float32)[16 - R:]
            else:
                edge = source[first + r, :16].astype(jnp.float32)[:R]
            pack_ref[pl.ds(r * R, R)] = edge
        if target.shape[0] > count * R:
            pack_ref[count * R:target.shape[0]] = jnp.zeros((target.shape[0] - count * R, pack_ref.shape[1]), jnp.float32)
        target[...] = pack_ref[:target.shape[0]].astype(jnp.bfloat16)

    loads[2].wait()
    loads[3].wait()
    for i, (ref, right) in enumerate(((k_ref, True), (v_ref, True), (k_ref, False), (v_ref, False))):
        pack(ref, 0, TH, right, side_ref.at[i])
    start_halo(WEST)
    start_halo(EAST)
    for i, piece in enumerate((NW, NE, SW, SE)):
        @pl.when(crossing[piece])
        def _(i=i, piece=piece):
            for n, ref in enumerate((k_ref, v_ref)):
                pack(ref, TH - R if piece in (NW, NE) else 0, R, piece in (NW, SW), corner_ref.at[2 * i + n])
        start_halo(piece, True)

    def clear(missing, refs):
        @pl.when(missing)
        def _():
            for ref in refs:
                ref[...] = jnp.zeros(ref.shape, ref.dtype)

    top, middle, bottom = pl.ds(0, CORNER), pl.ds(CORNER, SIDE), pl.ds(CORNER + SIDE, CORNER)
    clear(jnp.logical_not(has_n), [kn_ref, vn_ref])
    clear(jnp.logical_not(has_s), [ks_ref, vs_ref])
    clear(jnp.logical_not(has_w), [kw_ref.at[middle], vw_ref.at[middle]])
    clear(jnp.logical_not(has_e), [ke_ref.at[middle], ve_ref.at[middle]])
    clear(jnp.logical_not(exists[NW]), [kw_ref.at[top], vw_ref.at[top]])
    clear(jnp.logical_not(exists[SW]), [kw_ref.at[bottom], vw_ref.at[bottom]])
    clear(jnp.logical_not(exists[NE]), [ke_ref.at[top], ve_ref.at[top]])
    clear(jnp.logical_not(exists[SE]), [ke_ref.at[bottom], ve_ref.at[bottom]])

    def key_marks(keys, place):
        shape = (keys, HD)
        u, v, real = place(lax.broadcasted_iota(jnp.int32, shape, 0))
        lane = lax.broadcasted_iota(jnp.int32, shape, 1)
        on = (lane == u + R + ROW_AT) | (lane == v + R + COL_AT) | ((lane == PAD_AT) & jnp.logical_not(real))
        return jnp.where(on, 1.0, 0.0).astype(jnp.bfloat16)

    def make_query_marks():
        shape = (TH * TW, HD)
        query, lane = lax.broadcasted_iota(jnp.int32, shape, 0), lax.broadcasted_iota(jnp.int32, shape, 1)
        u, v = lane - ROW_AT - R, lane - COL_AT - R
        row_off = (jnp.abs(u - query // TW) > R) | (u + row * TH < 0) | (u + row * TH >= ROWS * TH)
        col_off = (jnp.abs(v - query % TW) > R) | (v + col * TW < 0) | (v + col * TW >= COLS * TW)
        low = ((lane < COL_AT) & row_off) | ((lane >= COL_AT) & (lane < PAD_AT) & col_off) | (lane == PAD_AT)
        return jnp.where(low, LOW, jnp.where(lane == DEAD_AT, 1.0, 0.0)).astype(jnp.bfloat16)

    def strip_place(first_col):
        def place(key):
            upper, lower = key < CORNER, key >= CORNER + SIDE
            start = jnp.where(upper, 0, jnp.where(lower, CORNER + SIDE, CORNER))
            first_row = jnp.where(upper, -R, jnp.where(lower, TH, 0))
            cell = key - start
            real = (cell < R * R) | jnp.logical_not(upper | lower)
            return first_row + cell // R, first_col + cell % R, real

        return place

    def band_place(first_row):
        return lambda key: (first_row + key // TW, key % TW, key >= 0)

    query_marks[...] = make_query_marks()
    own_marks[...] = key_marks(TH * TW, band_place(0))

    def lanes(h):
        return pl.ds(pl.multiple_of(h * HD, HD), HD)

    def across(half):
        return pl.ds(half * HALF, HALF)

    def scores(keys, query):
        return lax.dot_general(keys, query, (((1,), (1,)), ((), ())), preferred_element_type=jnp.float32)

    def mix(values, weights):
        return lax.dot_general(values, weights, (((0,), (0,)), ((), ())), preferred_element_type=jnp.float32)

    def absorb(h0, parts_of, first=False):
        chains = [(h0 + i, half) for i in (0, 1) for half in (0, 1)]

        def start(chain):
            h, half = chain
            query = jnp.concatenate([q_ref[across(half), lanes(h)], query_marks[across(half)]], axis=1)
            parts = parts_of(h, half)
            return [(scores(jnp.concatenate([keys, marks], axis=1), query), values) for keys, marks, values in parts]

        def finish(chain, parts):
            h, half = chain
            peak = jnp.max(parts[0][0], axis=0, keepdims=True)
            for raw, _ in parts[1:]:
                peak = jnp.maximum(peak, jnp.max(raw, axis=0, keepdims=True))
            if not first:
                before = m_ref[h, :, across(half)]
                peak = jnp.maximum(before, peak)
            total, mixed = None, None
            for raw, values in parts:
                weights = jnp.exp2((raw - peak) * SCALE)
                part = jnp.sum(weights, axis=0, keepdims=True)
                product = mix(values, weights.astype(jnp.bfloat16))
                total = part if total is None else total + part
                mixed = product if mixed is None else mixed + product
            if not first:
                fade = jnp.exp2((before - peak) * SCALE)
                total = l_ref[h, :, across(half)] * fade + total
                mixed = acc_ref[h, :, across(half)] * fade + mixed
            return peak, total, mixed

        results = []
        ready = start(chains[0])
        for n, chain in enumerate(chains):
            parts = ready
            if n + 1 < len(chains):
                ready = start(chains[n + 1])
            results.append(finish(chain, parts))
        for (h, half), found in zip(chains, results):
            m_ref[h, :, across(half)], l_ref[h, :, across(half)], acc_ref[h, :, across(half)] = found

    loads[4].wait()

    @pl.loop(0, heads, step=2)
    def _(h0):
        @pl.loop(0, 2 * EARLY)
        def _(j):
            send_main(h0 * EARLY + j)

        def parts_of(h, half):
            rows = pl.ds(half * 2, TH - 2)
            keys = k_ref[rows, :, lanes(h)].reshape(OWN_SPAN, HD)
            return [(keys, own_marks[pl.ds(half * 2 * TW, OWN_SPAN)], v_ref[rows, :, lanes(h)].reshape(OWN_SPAN, HD))]

        absorb(h0, parts_of, first=True)

    west_marks[...] = key_marks(STRIP, strip_place(-R))
    east_marks[...] = key_marks(STRIP, strip_place(TW))
    north_marks[...] = key_marks(BAND, band_place(-R))
    south_marks[...] = key_marks(BAND, band_place(TH))

    def far_sources():
        slot = lax.broadcasted_iota(jnp.int32, (far_lists.shape[0], SLOTS), 1)
        found = [
            jnp.where(slot < CLOSE, first, jnp.where(slot < MAIN, second, third))
            for first, second, third in zip(close_offset(slot), edge_offset(slot - CLOSE), main_offset(slot - MAIN))
        ]
        source = tile_at(row, col, *(-part for part in found))
        return jnp.where(slot == UNUSED, -2, source[0] * COLS + source[1]).astype(jnp.float32)

    tile = lax.broadcasted_iota(jnp.int32, far_lists.shape, 1)
    own_list = jnp.max(jnp.where(tile == row * COLS + col, far_lists[...].astype(jnp.float32), -1.0), axis=1, keepdims=True)
    listed = jnp.max(jnp.where(far_sources() == own_list, 0.0, LOW).astype(jnp.float32), axis=0, keepdims=True)
    live_ref[...] = jnp.broadcast_to(listed, live_ref.shape).T

    @pl.loop(0, SLOTS // 2)
    def _(pair):
        both = [jnp.broadcast_to(live_ref[pl.ds(2 * pair + i, 1), :], (BLK, HD)) for i in (0, 1)]
        lane = lax.broadcasted_iota(jnp.int32, (2 * BLK, HD), 1)
        marks = jnp.where(lane == DEAD_AT, jnp.concatenate(both, axis=0), 0.0)
        far_marks[pl.ds(pl.multiple_of(pair * 2 * BLK, 2 * BLK), 2 * BLK)] = marks.astype(jnp.bfloat16)

    def use_far(group):
        first, count = GROUPS[group]
        regular = CLOSE + GROUPS[1][0] - MAIN if group == 0 else count
        part = far_ref.at[pl.ds(first, regular)]
        pltpu.make_async_remote_copy(
            src_ref=part, dst_ref=part, send_sem=far_send, recv_sem=far_recv.at[group],
            device_id=(row, (col + 1) % COLS), device_id_type=MESH,
        ).wait_recv()
        if group == 0:
            for i in range(len(EDGE)):
                _, _, receives, copy = edge(i)

                @pl.when(receives)
                def _(copy=copy):
                    copy.wait_recv()

        @pl.loop(0, heads, step=2)
        def _(h0):
            def parts_of(h, half):
                both = far_ref[pl.ds(first, count), :, lanes(h)].astype(jnp.float32)
                keys = both[:, :BLK].reshape(count * BLK, HD).astype(jnp.bfloat16)
                values = both[:, BLK:].reshape(count * BLK, HD).astype(jnp.bfloat16)
                return [(keys, far_marks[pl.ds(first * BLK, count * BLK)], values)]

            absorb(h0, parts_of)

    use_far(0)
    wait_halo(NORTH)
    wait_halo(SOUTH)
    for i, piece in enumerate((NW, NE, SW, SE)):
        @pl.when(jnp.logical_not(crossing[piece]))
        def _(i=i, piece=piece):
            for n, ref in enumerate((kn_ref, vn_ref) if piece in (NW, NE) else (ks_ref, vs_ref)):
                pack(ref, 0, R, piece in (NW, SW), corner_ref.at[2 * i + n])
        start_halo(piece)

    wait_halo(WEST)
    wait_halo(EAST)

    @pl.loop(0, heads, step=2)
    def _(h0):
        @pl.loop(0, 2 * LATE)
        def _(j):
            send_main(heads * EARLY + h0 * LATE + j)

        def parts_of(h, half):
            band_k, band_v, marks = ((kn_ref, vn_ref, north_marks), (ks_ref, vs_ref, south_marks))[half]
            found = [(band_k[:, :, lanes(h)].reshape(BAND, HD), marks[...], band_v[:, :, lanes(h)].reshape(BAND, HD))]
            for strip_k, strip_v, marks in ((kw_ref, vw_ref, west_marks), (ke_ref, ve_ref, east_marks)):
                found.append((strip_k[middle, lanes(h)], marks[middle], strip_v[middle, lanes(h)]))
            return found

        absorb(h0, parts_of)

    use_far(1)
    use_far(2)
    for piece in (NW, NE, SW, SE):
        wait_halo(piece)

    @pl.loop(0, heads, step=2)
    def _(h0):
        def parts_of(h, half):
            end = (top, bottom)[half]
            return [
                (strip_k[end, lanes(h)], marks[end], strip_v[end, lanes(h)])
                for strip_k, strip_v, marks in ((kw_ref, vw_ref, west_marks), (ke_ref, ve_ref, east_marks))
            ]

        absorb(h0, parts_of)

    use_far(3)

    @pl.loop(0, heads)
    def _(h):
        att_ref[:, lanes(h)] = (acc_ref[h] / l_ref[h]).T.astype(jnp.bfloat16)

    out_copy = pltpu.make_async_copy(att_ref, att_hbm, out_sem)
    out_copy.start()

    for piece in range(8):
        wait_halo_sent(piece)
        if piece in crossing:
            wait_halo_sent(piece, True)
    sent = stage_ref.at[pl.ds(0, CLOSE + N_MAIN)]
    pltpu.make_async_remote_copy(
        src_ref=sent, dst_ref=sent, send_sem=far_send, recv_sem=far_recv.at[0],
        device_id=(row, (col + 1) % COLS), device_id_type=MESH,
    ).wait_send()
    for i in range(len(EDGE)):
        _, sends, _, copy = edge(i)

        @pl.when(sends)
        def _(copy=copy):
            copy.wait_send()
    out_copy.wait()


def shards(
    queries, fresh_keys, fresh_values, stale_keys, stale_values, weight_out, gate, far_tiles, far_blocks, far_count
):
    inner = queries.shape[2]
    heads = inner // HD
    model = weight_out.shape[1]
    own = lax.axis_index("row") * COLS + lax.axis_index("col")
    block_of = jnp.sum(jnp.where(far_tiles == own, far_blocks, 0), axis=1)

    bf16, f32 = jnp.bfloat16, jnp.float32
    tokens = TH * TW
    any_spec = pl.BlockSpec(memory_space=pl.ANY)
    vmem_spec = pl.BlockSpec(memory_space=pltpu.VMEM)
    smem_spec = pl.BlockSpec(memory_space=pltpu.SMEM)
    band, strip = (R, TW, inner), (STRIP, inner)
    attended = pl.pallas_call(
        kernel,
        out_shape=jax.ShapeDtypeStruct((tokens, inner), bf16),
        in_specs=[any_spec] * 5 + [vmem_spec, smem_spec],
        out_specs=any_spec,
        scratch_shapes=[
            pltpu.VMEM((tokens, inner), bf16),
            pltpu.VMEM((TH, TW, inner), bf16),
            pltpu.VMEM((TH, TW, inner), bf16),
            pltpu.VMEM((tokens // 16, 16, inner), bf16),
            pltpu.VMEM((tokens // 16, 16, inner), bf16),
            pltpu.VMEM(band, bf16), pltpu.VMEM(band, bf16), pltpu.VMEM(strip, bf16), pltpu.VMEM(strip, bf16),
            pltpu.VMEM(band, bf16), pltpu.VMEM(band, bf16), pltpu.VMEM(strip, bf16), pltpu.VMEM(strip, bf16),
            pltpu.VMEM((SIDE, inner), f32),
            pltpu.VMEM((4, SIDE, inner), bf16),
            pltpu.VMEM((8, CORNER, inner), bf16),
            pltpu.VMEM((SLOTS, 2 * BLK, inner), bf16),
            pltpu.VMEM((SLOTS, 2 * BLK, inner), bf16),
            pltpu.VMEM((heads, HD, tokens), f32),
            pltpu.VMEM((heads, 1, tokens), f32),
            pltpu.VMEM((heads, 1, tokens), f32),
            pltpu.VMEM((tokens, HD), bf16),
            pltpu.VMEM((tokens, HD), bf16),
            pltpu.VMEM((BAND, HD), bf16),
            pltpu.VMEM((BAND, HD), bf16),
            pltpu.VMEM((STRIP, HD), bf16),
            pltpu.VMEM((STRIP, HD), bf16),
            pltpu.VMEM((SLOTS * BLK, HD), bf16),
            pltpu.VMEM((SLOTS, 128), f32),
            pltpu.VMEM((tokens, inner), bf16),
            pltpu.SemaphoreType.DMA((5,)),
            pltpu.SemaphoreType.DMA((16,)),
            pltpu.SemaphoreType.DMA((16,)),
            pltpu.SemaphoreType.DMA,
            pltpu.SemaphoreType.DMA((len(GROUPS),)),
            pltpu.SemaphoreType.DMA((len(EDGE),)),
            pltpu.SemaphoreType.DMA((len(EDGE),)),
            pltpu.SemaphoreType.DMA,
        ],
        compiler_params=pltpu.CompilerParams(has_side_effects=True, vmem_limit_bytes=57 * 1024 * 1024),
        name="attention",
    )(
        queries.reshape(tokens, inner), fresh_keys, fresh_values,
        stale_keys.reshape(-1, 16, inner), stale_values.reshape(-1, 16, inner), far_tiles.T, block_of,
    )
    projected = jnp.dot(attended, weight_out, preferred_element_type=jnp.float32)
    return (projected * gate[None, :]).astype(bf16).reshape(TH, TW, model)


def solution(mesh):
    tile = P("row", "col", None)
    return jax.shard_map(
        shards, mesh=mesh, in_specs=(tile,) * 5 + (P(),) * 5, out_specs=tile, check_vma=False,
    )
```

time: 292 us -> 169 us (0.58)
  the two profiles are of different devices: /device:TPU:26 before, /device:TPU:5 now
where the time goes in v1:
time: 169 us
  Pallas kernels  159 us (94%)
  matrix products  9.23 us (5%)
    pallas_call x1, Pallas kernels, shards(): pl.pallas_call(kernel, out_shape=jax.ShapeDtypeStruct((tokens, inner), bf...  159 us
    dot_general x1, matrix products, shards(): jnp.dot(attended, weight_out, preferred_element_type=jnp.float32)  9.23 us

profile of v1, /device:TPU:5, one launch (start us, length us, event | category | flops | bytes accessed | tf_op | source)
XLA Modules:
  0.0 169.1 jit_solution(13529655550598200230)
XLA Ops:
  0.0 1.3 select_reduce_fusion.block_of
  1.3 0.0 copy-start
  1.3 158.5 %attention.1 = bf16[512,1536]{1,0:T(8,128)(2,1)} custom-call(bf16[512,1536]{1,0:T(8,128)(2,1)} %bitcast.7, bf16[16,32,1536]{2,1,0:T(8,128)(2,1)} %k_hbm.1, bf16[16,32,1536]{2,1,0:T(8,128)(2,1)} %v_hbm.1, bf16[32,16,1536]{2,1,0:T(8,128)(2,1)} %bitcast.8, bf16[32,16,1536]{2,1,0:T(8,128)(2,1)} %bitcast.9, s32[80,128]{1,0:T(8,128)} %bitcast.10, ...), custom_call_target="tpu_custom_call" | custom-call | tf_op jit(solution)/shard_map/attention/pallas_call | solution.py:495
  159.9 0.0 copy-done
  159.9 9.2 %multiply_convert_fusion = bf16[512,3072]{1,0:T(8,128)(2,1)} fusion(bf16[512,1536]{1,0:T(8,128)(2,1)} %attention.1, bf16[1536,3072]{1,0:T(8,128)(2,1)} %param.15, f32[3072]{0:T(1024)S(1)} %copy-done), kind=kOutput, calls=%fused_computation | convolution fusion | flops 4834983936 | bytes 14168064 | tf_op jit(solution)/shard_map/dot_general | solution.py:540
Async XLA Ops:
  1.3 158.5 %copy-start = (f32[3072]{0:T(1024)S(1)}, f32[3072]{0:T(1024)}, u32[]{:S(2)}) copy-start(f32[3072]{0:T(1024)} %param.16) | copy-start | bytes 36868

commit v2 on v1

--- a/solution.py
+++ b/solution.py
@@ -26,7 +26,7 @@
 N_MAIN = SLOTS - MAIN
 MID = COLS // 2
 GROUPS = ((0, 48), (48, 32), (80, 32), (112, 16))
-EARLY, LATE = 3, 4
+EARLY, LATE = 4, 36
 
 
 def blend(late, before, after):
@@ -75,7 +75,7 @@
     q_ref, k_ref, v_ref, sk_ref, sv_ref,
     kn_ref, ks_ref, kw_ref, ke_ref, vn_ref, vs_ref, vw_ref, ve_ref,
     pack_ref, side_ref, corner_ref,
-    far_ref, stage_ref, acc_ref, m_ref, l_ref, query_marks, own_marks, north_marks, south_marks, west_marks, east_marks, far_marks,
+    far_ref, stage_ref, acc_ref, m_ref, l_ref, qt_ref, far_k, far_v, own_marks, north_marks, south_marks, west_marks, east_marks, far_marks,
     live_ref, att_ref,
     load_sem, halo_send, halo_recv, far_send, far_recv, edge_send, edge_recv, out_sem,
 ):
@@ -262,8 +262,8 @@
         return jnp.where(on, 1.0, 0.0).astype(jnp.bfloat16)
 
     def make_query_marks():
-        shape = (TH * TW, HD)
-        query, lane = lax.broadcasted_iota(jnp.int32, shape, 0), lax.broadcasted_iota(jnp.int32, shape, 1)
+        shape = (HD, TH * TW)
+        lane, query = lax.broadcasted_iota(jnp.int32, shape, 0), lax.broadcasted_iota(jnp.int32, shape, 1)
         u, v = lane - ROW_AT - R, lane - COL_AT - R
         row_off = (jnp.abs(u - query // TW) > R) | (u + row * TH < 0) | (u + row * TH >= ROWS * TH)
         col_off = (jnp.abs(v - query % TW) > R) | (v + col * TW < 0) | (v + col * TW >= COLS * TW)
@@ -284,27 +284,26 @@
     def band_place(first_row):
         return lambda key: (first_row + key // TW, key % TW, key >= 0)
 
-    query_marks[...] = make_query_marks()
     own_marks[...] = key_marks(TH * TW, band_place(0))
 
     def lanes(h):
         return pl.ds(pl.multiple_of(h * HD, HD), HD)
 
     def across(half):
-        return pl.ds(half * HALF, HALF)
+        return pl.ds(0, 2 * HALF) if half is None else pl.ds(half * HALF, HALF)
 
     def scores(keys, query):
-        return lax.dot_general(keys, query, (((1,), (1,)), ((), ())), preferred_element_type=jnp.float32)
+        return jnp.dot(keys, query, preferred_element_type=jnp.float32)
 
     def mix(values, weights):
         return lax.dot_general(values, weights, (((0,), (0,)), ((), ())), preferred_element_type=jnp.float32)
 
-    def absorb(h0, parts_of, first=False):
-        chains = [(h0 + i, half) for i in (0, 1) for half in (0, 1)]
+    def absorb(h0, parts_of, first=False, halves=(0, 1)):
+        chains = [(h0 + i, half) for i in (0, 1) for half in halves]
 
         def start(chain):
             h, half = chain
-            query = jnp.concatenate([q_ref[across(half), lanes(h)], query_marks[across(half)]], axis=1)
+            query = qt_ref[h, :, across(half)]
             parts = parts_of(h, half)
             return [(scores(jnp.concatenate([keys, marks], axis=1), query), values) for keys, marks, values in parts]
 
@@ -340,6 +339,12 @@
             m_ref[h, :, across(half)], l_ref[h, :, across(half)], acc_ref[h, :, across(half)] = found
 
     loads[4].wait()
+    marks_t = make_query_marks()
+
+    @pl.loop(0, heads)
+    def _(h):
+        qt_ref[h, :HD] = q_ref[:, lanes(h)].astype(jnp.float32).T.astype(jnp.bfloat16)
+        qt_ref[h, HD:] = marks_t
 
     @pl.loop(0, heads, step=2)
     def _(h0):
@@ -396,17 +401,20 @@
                 def _(copy=copy):
                     copy.wait_recv()
 
+        @pl.loop(first // 2, (first + count) // 2)
+        def _(pair):
+            rows = pl.ds(pl.multiple_of(pair * 2 * BLK, 2 * BLK), 2 * BLK)
+            one, two = far_ref[2 * pair].astype(jnp.float32), far_ref[2 * pair + 1].astype(jnp.float32)
+            far_k[rows] = jnp.concatenate([one[:BLK], two[:BLK]], axis=0).astype(jnp.bfloat16)
+            far_v[rows] = jnp.concatenate([one[BLK:], two[BLK:]], axis=0).astype(jnp.bfloat16)
+
         @pl.loop(0, heads, step=2)
         def _(h0):
-            def parts_of(h, half):
-                both = far_ref[pl.ds(first, count), :, lanes(h)].astype(jnp.float32)
-                keys = both[:, :BLK].reshape(count * BLK, HD).astype(jnp.bfloat16)
-                values = both[:, BLK:].reshape(count * BLK, HD).astype(jnp.bfloat16)
-                return [(keys, far_marks[pl.ds(first * BLK, count * BLK)], values)]
-
-            absorb(h0, parts_of)
+            rows = pl.ds(first * BLK, count * BLK)
+            absorb(h0, lambda h, half: [(far_k[rows, lanes(h)], far_marks[rows], far_v[rows, lanes(h)])], halves=(None,))
 
     use_far(0)
+    use_far(1)
     wait_halo(NORTH)
     wait_halo(SOUTH)
     for i, piece in enumerate((NW, NE, SW, SE)):
@@ -416,15 +424,15 @@
                 pack(ref, 0, R, piece in (NW, SW), corner_ref.at[2 * i + n])
         start_halo(piece)
 
+    @pl.loop(heads * EARLY, heads * EARLY + LATE)
+    def _(p):
+        send_main(p)
+
     wait_halo(WEST)
     wait_halo(EAST)
 
     @pl.loop(0, heads, step=2)
     def _(h0):
-        @pl.loop(0, 2 * LATE)
-        def _(j):
-            send_main(heads * EARLY + h0 * LATE + j)
-
         def parts_of(h, half):
             band_k, band_v, marks = ((kn_ref, vn_ref, north_marks), (ks_ref, vs_ref, south_marks))[half]
             found = [(band_k[:, :, lanes(h)].reshape(BAND, HD), marks[...], band_v[:, :, lanes(h)].reshape(BAND, HD))]
@@ -434,7 +442,6 @@
 
         absorb(h0, parts_of)
 
-    use_far(1)
     use_far(2)
     for piece in (NW, NE, SW, SE):
         wait_halo(piece)
@@ -513,7 +520,9 @@
             pltpu.VMEM((heads, HD, tokens), f32),
             pltpu.VMEM((heads, 1, tokens), f32),
             pltpu.VMEM((heads, 1, tokens), f32),
-            pltpu.VMEM((tokens, HD), bf16),
+            pltpu.VMEM((heads, 2 * HD, tokens), bf16),
+            pltpu.VMEM((SLOTS * BLK, inner), bf16),
+            pltpu.VMEM((SLOTS * BLK, inner), bf16),
             pltpu.VMEM((tokens, HD), bf16),
             pltpu.VMEM((BAND, HD), bf16),
             pltpu.VMEM((BAND, HD), bf16),
@@ -531,7 +540,7 @@
             pltpu.SemaphoreType.DMA((len(EDGE),)),
             pltpu.SemaphoreType.DMA,
         ],
-        compiler_params=pltpu.CompilerParams(has_side_effects=True, vmem_limit_bytes=57 * 1024 * 1024),
+        compiler_params=pltpu.CompilerParams(has_side_effects=True, vmem_limit_bytes=52 * 1024 * 1024),
         name="attention",
     )(
         queries.reshape(tokens, inner), fresh_keys, fresh_values,

time: 169 us -> 167 us (0.988)
  the two profiles are of different devices: /device:TPU:5 before, /device:TPU:8 now
where the time goes in v2:
time: 167 us
  Pallas kernels  159 us (95%)
  matrix products  6.4 us (4%)
    pallas_call x1, Pallas kernels, shards(): pl.pallas_call(kernel, out_shape=jax.ShapeDtypeStruct((tokens, inner), bf...  159 us
    dot_general x1, matrix products, shards(): jnp.dot(attended, weight_out, preferred_element_type=jnp.float32)  6.4 us

profile of v2, /device:TPU:8, one launch (start us, length us, event | category | flops | bytes accessed | tf_op | source)
XLA Modules:
  0.0 166.7 jit_solution(12009309325339817596)
XLA Ops:
  0.0 0.8 select_reduce_fusion.block_of
  0.8 0.0 copy-start
  0.8 0.8 copy-done
  1.6 0.0 copy-start.1
  1.6 0.0 copy-start.2
  1.6 158.7 %attention.1 = bf16[512,1536]{1,0:T(8,128)(2,1)S(1)} custom-call(bf16[512,1536]{1,0:T(8,128)(2,1)} %bitcast.8, bf16[16,32,1536]{2,1,0:T(8,128)(2,1)} %k_hbm.1, bf16[16,32,1536]{2,1,0:T(8,128)(2,1)} %v_hbm.1, bf16[32,16,1536]{2,1,0:T(8,128)(2,1)} %bitcast.9, bf16[32,16,1536]{2,1,0:T(8,128)(2,1)} %bitcast.10, s32[80,128]{1,0:T(8,128)S(1)} %bitcast.7, ...), custom_call_target="tpu_custom_call" | custom-call | tf_op jit(solution)/shard_map/attention/pallas_call | solution.py:502
  160.3 0.0 copy-done.1
  160.3 0.0 copy-done.2
  160.3 6.4 %multiply_convert_fusion = bf16[512,3072]{1,0:T(8,128)(2,1)} fusion(bf16[512,1536]{1,0:T(8,128)(2,1)S(1)} %attention.1, bf16[1536,3072]{1,0:T(8,128)(2,1)S(1)} %copy-done.1, f32[3072]{0:T(1024)S(1)} %copy-done.2), kind=kOutput, calls=%fused_computation | convolution fusion | flops 4834983936 | bytes 14168064 | tf_op jit(solution)/shard_map/dot_general | solution.py:549
Async XLA Ops:
  0.8 0.8 copy-start
  1.6 158.7 %copy-start.1 = (bf16[1536,3072]{1,0:T(8,128)(2,1)S(1)}, bf16[1536,3072]{1,0:T(8,128)(2,1)}, u32[]{:S(2)}) copy-start(bf16[1536,3072]{1,0:T(8,128)(2,1)} %param.15) | copy-start | bytes 28311556
  1.6 158.7 %copy-start.2 = (f32[3072]{0:T(1024)S(1)}, f32[3072]{0:T(1024)}, u32[]{:S(2)}) copy-start(f32[3072]{0:T(1024)} %param.16) | copy-start | bytes 36868

commit v3 on v2

--- a/solution.py
+++ b/solution.py
@@ -26,7 +26,7 @@
 N_MAIN = SLOTS - MAIN
 MID = COLS // 2
 GROUPS = ((0, 48), (48, 32), (80, 32), (112, 16))
-EARLY, LATE = 4, 36
+EARLY = 4
 
 
 def blend(late, before, after):
@@ -191,6 +191,9 @@
     def send_main(p):
         send_far(MAIN + p, main_offset(p), (MAIN + p - 16) // 32)
 
+    for p in range(EARLY):
+        send_main(p)
+
     def touches(dr, other):
         return (row + dr >= 0) & (row + dr < ROWS) & (other[1] - col >= -1) & (other[1] - col <= 1)
 
@@ -254,24 +257,26 @@
     clear(jnp.logical_not(exists[NE]), [ke_ref.at[top], ve_ref.at[top]])
     clear(jnp.logical_not(exists[SE]), [ke_ref.at[bottom], ve_ref.at[bottom]])
 
-    def key_marks(keys, place):
-        shape = (keys, HD)
-        u, v, real = place(lax.broadcasted_iota(jnp.int32, shape, 0))
-        lane = lax.broadcasted_iota(jnp.int32, shape, 1)
+    def key_marks(shape, place):
+        u, v, real = place(shape)
+        lane = lax.broadcasted_iota(jnp.int32, shape, len(shape) - 1)
         on = (lane == u + R + ROW_AT) | (lane == v + R + COL_AT) | ((lane == PAD_AT) & jnp.logical_not(real))
-        return jnp.where(on, 1.0, 0.0).astype(jnp.bfloat16)
+        return jnp.where(on, 1.0, 0.0).reshape(-1, HD).astype(jnp.bfloat16)
 
     def make_query_marks():
         shape = (HD, TH * TW)
-        lane, query = lax.broadcasted_iota(jnp.int32, shape, 0), lax.broadcasted_iota(jnp.int32, shape, 1)
+        lane = lax.broadcasted_iota(jnp.int32, shape, 0)
+        query = lax.broadcasted_iota(jnp.int32, (1, TH * TW), 1)
+        query_row, query_col = query // TW, query % TW
         u, v = lane - ROW_AT - R, lane - COL_AT - R
-        row_off = (jnp.abs(u - query // TW) > R) | (u + row * TH < 0) | (u + row * TH >= ROWS * TH)
-        col_off = (jnp.abs(v - query % TW) > R) | (v + col * TW < 0) | (v + col * TW >= COLS * TW)
+        row_off = (jnp.abs(u - query_row) > R) | (u + row * TH < 0) | (u + row * TH >= ROWS * TH)
+        col_off = (jnp.abs(v - query_col) > R) | (v + col * TW < 0) | (v + col * TW >= COLS * TW)
         low = ((lane < COL_AT) & row_off) | ((lane >= COL_AT) & (lane < PAD_AT) & col_off) | (lane == PAD_AT)
         return jnp.where(low, LOW, jnp.where(lane == DEAD_AT, 1.0, 0.0)).astype(jnp.bfloat16)
 
     def strip_place(first_col):
-        def place(key):
+        def place(shape):
+            key = lax.broadcasted_iota(jnp.int32, shape, 0)
             upper, lower = key < CORNER, key >= CORNER + SIDE
             start = jnp.where(upper, 0, jnp.where(lower, CORNER + SIDE, CORNER))
             first_row = jnp.where(upper, -R, jnp.where(lower, TH, 0))
@@ -282,9 +287,13 @@
         return place
 
     def band_place(first_row):
-        return lambda key: (first_row + key // TW, key % TW, key >= 0)
-
-    own_marks[...] = key_marks(TH * TW, band_place(0))
+        def place(shape):
+            u, v = (lax.broadcasted_iota(jnp.int32, shape, axis) for axis in (0, 1))
+            return first_row + u, v, v >= 0
+
+        return place
+
+    own_marks[...] = key_marks((TH, TW, HD), band_place(0))
 
     def lanes(h):
         return pl.ds(pl.multiple_of(h * HD, HD), HD)
@@ -298,7 +307,7 @@
     def mix(values, weights):
         return lax.dot_general(values, weights, (((0,), (0,)), ((), ())), preferred_element_type=jnp.float32)
 
-    def absorb(h0, parts_of, first=False, halves=(0, 1)):
+    def absorb(h0, parts_of, first=False, halves=(0, 1), last=False):
         chains = [(h0 + i, half) for i in (0, 1) for half in halves]
 
         def start(chain):
@@ -335,6 +344,10 @@
             if n + 1 < len(chains):
                 ready = start(chains[n + 1])
             results.append(finish(chain, parts))
+        if last:
+            for (h, half), (_, total, mixed) in zip(chains, results):
+                att_ref[across(half), lanes(h)] = (mixed / total).T.astype(jnp.bfloat16)
+            return
         for (h, half), found in zip(chains, results):
             m_ref[h, :, across(half)], l_ref[h, :, across(half)], acc_ref[h, :, across(half)] = found
 
@@ -348,10 +361,6 @@
 
     @pl.loop(0, heads, step=2)
     def _(h0):
-        @pl.loop(0, 2 * EARLY)
-        def _(j):
-            send_main(h0 * EARLY + j)
-
         def parts_of(h, half):
             rows = pl.ds(half * 2, TH - 2)
             keys = k_ref[rows, :, lanes(h)].reshape(OWN_SPAN, HD)
@@ -359,13 +368,13 @@
 
         absorb(h0, parts_of, first=True)
 
-    west_marks[...] = key_marks(STRIP, strip_place(-R))
-    east_marks[...] = key_marks(STRIP, strip_place(TW))
-    north_marks[...] = key_marks(BAND, band_place(-R))
-    south_marks[...] = key_marks(BAND, band_place(TH))
+    west_marks[...] = key_marks((STRIP, HD), strip_place(-R))
+    east_marks[...] = key_marks((STRIP, HD), strip_place(TW))
+    north_marks[...] = key_marks((R, TW, HD), band_place(-R))
+    south_marks[...] = key_marks((R, TW, HD), band_place(TH))
 
     def far_sources():
-        slot = lax.broadcasted_iota(jnp.int32, (far_lists.shape[0], SLOTS), 1)
+        slot = lax.broadcasted_iota(jnp.int32, (1, SLOTS), 1)
         found = [
             jnp.where(slot < CLOSE, first, jnp.where(slot < MAIN, second, third))
             for first, second, third in zip(close_offset(slot), edge_offset(slot - CLOSE), main_offset(slot - MAIN))
@@ -411,10 +420,10 @@
         @pl.loop(0, heads, step=2)
         def _(h0):
             rows = pl.ds(first * BLK, count * BLK)
-            absorb(h0, lambda h, half: [(far_k[rows, lanes(h)], far_marks[rows], far_v[rows, lanes(h)])], halves=(None,))
+            absorb(h0, lambda h, half: [(far_k[rows, lanes(h)], far_marks[rows], far_v[rows, lanes(h)])],
+                   halves=(None,), last=group == len(GROUPS) - 1)
 
     use_far(0)
-    use_far(1)
     wait_halo(NORTH)
     wait_halo(SOUTH)
     for i, piece in enumerate((NW, NE, SW, SE)):
@@ -424,7 +433,7 @@
                 pack(ref, 0, R, piece in (NW, SW), corner_ref.at[2 * i + n])
         start_halo(piece)
 
-    @pl.loop(heads * EARLY, heads * EARLY + LATE)
+    @pl.loop(EARLY, N_MAIN)
     def _(p):
         send_main(p)
 
@@ -442,6 +451,7 @@
 
         absorb(h0, parts_of)
 
+    use_far(1)
     use_far(2)
     for piece in (NW, NE, SW, SE):
         wait_halo(piece)
@@ -458,10 +468,6 @@
         absorb(h0, parts_of)
 
     use_far(3)
-
-    @pl.loop(0, heads)
-    def _(h):
-        att_ref[:, lanes(h)] = (acc_ref[h] / l_ref[h]).T.astype(jnp.bfloat16)
 
     out_copy = pltpu.make_async_copy(att_ref, att_hbm, out_sem)
     out_copy.start()

time: 167 us -> 158 us (0.946)
  the two profiles are of different devices: /device:TPU:8 before, /device:TPU:1 now
where the time goes in v3:
time: 158 us; the launch traced here: 157 us
  Pallas kernels  149 us (94%)
  matrix products  6.4 us (4%)
    pallas_call x1, Pallas kernels, shards(): pl.pallas_call(kernel, out_shape=jax.ShapeDtypeStruct((tokens, inner), bf...  149 us
    dot_general x1, matrix products, shards(): jnp.dot(attended, weight_out, preferred_element_type=jnp.float32)  6.4 us

profile of v3, /device:TPU:1, one launch (start us, length us, event | category | flops | bytes accessed | tf_op | source)
XLA Modules:
  0.0 157.5 jit_solution(11460373079347537461)
XLA Ops:
  0.0 0.8 select_reduce_fusion.block_of
  0.8 0.0 copy-start
  0.8 0.8 copy-done
  1.6 0.0 copy-start.1
  1.6 0.0 copy-start.2
  1.6 149.4 %attention.1 = bf16[512,1536]{1,0:T(8,128)(2,1)S(1)} custom-call(bf16[512,1536]{1,0:T(8,128)(2,1)} %bitcast.8, bf16[16,32,1536]{2,1,0:T(8,128)(2,1)} %k_hbm.1, bf16[16,32,1536]{2,1,0:T(8,128)(2,1)} %v_hbm.1, bf16[32,16,1536]{2,1,0:T(8,128)(2,1)} %bitcast.9, bf16[32,16,1536]{2,1,0:T(8,128)(2,1)} %bitcast.10, s32[80,128]{1,0:T(8,128)S(1)} %bitcast.7, ...), custom_call_target="tpu_custom_call" | custom-call | tf_op jit(solution)/shard_map/attention/pallas_call | solution.py:508
  151.0 0.0 copy-done.1
  151.0 0.0 copy-done.2
  151.1 6.4 %multiply_convert_fusion = bf16[512,3072]{1,0:T(8,128)(2,1)} fusion(bf16[512,1536]{1,0:T(8,128)(2,1)S(1)} %attention.1, bf16[1536,3072]{1,0:T(8,128)(2,1)S(1)} %copy-done.1, f32[3072]{0:T(1024)S(1)} %copy-done.2), kind=kOutput, calls=%fused_computation | convolution fusion | flops 4834983936 | bytes 14168064 | tf_op jit(solution)/shard_map/dot_general | solution.py:555
Async XLA Ops:
  0.8 0.8 copy-start
  1.6 149.4 %copy-start.1 = (bf16[1536,3072]{1,0:T(8,128)(2,1)S(1)}, bf16[1536,3072]{1,0:T(8,128)(2,1)}, u32[]{:S(2)}) copy-start(bf16[1536,3072]{1,0:T(8,128)(2,1)} %param.15) | copy-start | bytes 28311556
  1.6 149.4 %copy-start.2 = (f32[3072]{0:T(1024)S(1)}, f32[3072]{0:T(1024)}, u32[]{:S(2)}) copy-start(f32[3072]{0:T(1024)} %param.16) | copy-start | bytes 36868

commit v4 on v3

--- a/solution.py
+++ b/solution.py
@@ -25,8 +25,8 @@
 SLOTS = 128
 N_MAIN = SLOTS - MAIN
 MID = COLS // 2
-GROUPS = ((0, 48), (48, 32), (80, 32), (112, 16))
-EARLY = 4
+GROUPS = ((0, MAIN), (MAIN, 32), (76, 32), (108, 20))
+AHEAD = 5
 
 
 def blend(late, before, after):
@@ -184,15 +184,12 @@
     loads[0].wait()
     loads[1].wait()
 
-    @pl.loop(0, CLOSE)
+    @pl.loop(0, AHEAD)
     def _(j):
         send_far(j, close_offset(j), 0)
 
     def send_main(p):
-        send_far(MAIN + p, main_offset(p), (MAIN + p - 16) // 32)
-
-    for p in range(EARLY):
-        send_main(p)
+        send_far(MAIN + p, main_offset(p), 1 + p // 32)
 
     def touches(dr, other):
         return (row + dr >= 0) & (row + dr < ROWS) & (other[1] - col >= -1) & (other[1] - col <= 1)
@@ -361,6 +358,11 @@
 
     @pl.loop(0, heads, step=2)
     def _(h0):
+        @pl.loop(0, 4)
+        def _(j):
+            slot = AHEAD + 2 * h0 + j
+            send_far(slot, close_offset(slot), 0)
+
         def parts_of(h, half):
             rows = pl.ds(half * 2, TH - 2)
             keys = k_ref[rows, :, lanes(h)].reshape(OWN_SPAN, HD)
@@ -396,7 +398,7 @@
 
     def use_far(group):
         first, count = GROUPS[group]
-        regular = CLOSE + GROUPS[1][0] - MAIN if group == 0 else count
+        regular = CLOSE if group == 0 else count
         part = far_ref.at[pl.ds(first, regular)]
         pltpu.make_async_remote_copy(
             src_ref=part, dst_ref=part, send_sem=far_send, recv_sem=far_recv.at[group],
@@ -433,7 +435,7 @@
                 pack(ref, 0, R, piece in (NW, SW), corner_ref.at[2 * i + n])
         start_halo(piece)
 
-    @pl.loop(EARLY, N_MAIN)
+    @pl.loop(0, N_MAIN)
     def _(p):
         send_main(p)
 

time: 158 us -> 162 us (1.025)
  Pallas kernels: 149 us -> 153 us
    pallas_call x1, Pallas kernels: 149 us -> 153 us  [shards(): pl.pallas_call(kernel, out_shape=jax.ShapeDtypeStruct((tokens, inner), bf...]
where the time goes in v4:
time: 162 us; the launch traced here: 161 us
  Pallas kernels  153 us (94%)
  matrix products  6.4 us (4%)
    pallas_call x1, Pallas kernels, shards(): pl.pallas_call(kernel, out_shape=jax.ShapeDtypeStruct((tokens, inner), bf...  153 us
    dot_general x1, matrix products, shards(): jnp.dot(attended, weight_out, preferred_element_type=jnp.float32)  6.4 us

profile of v4, /device:TPU:1, one launch (start us, length us, event | category | flops | bytes accessed | tf_op | source)
XLA Modules:
  0.0 161.4 jit_solution(2949893425420894305)
XLA Ops:
  0.0 0.8 select_reduce_fusion.block_of
  0.8 0.0 copy-start
  0.8 0.8 copy-done
  1.6 0.0 copy-start.1
  1.6 0.0 copy-start.2
  1.6 153.4 %attention.1 = bf16[512,1536]{1,0:T(8,128)(2,1)S(1)} custom-call(bf16[512,1536]{1,0:T(8,128)(2,1)} %bitcast.8, bf16[16,32,1536]{2,1,0:T(8,128)(2,1)} %k_hbm.1, bf16[16,32,1536]{2,1,0:T(8,128)(2,1)} %v_hbm.1, bf16[32,16,1536]{2,1,0:T(8,128)(2,1)} %bitcast.9, bf16[32,16,1536]{2,1,0:T(8,128)(2,1)} %bitcast.10, s32[80,128]{1,0:T(8,128)S(1)} %bitcast.7, ...), custom_call_target="tpu_custom_call" | custom-call | tf_op jit(solution)/shard_map/attention/pallas_call | solution.py:510
  155.0 0.0 copy-done.1
  155.0 0.0 copy-done.2
  155.0 6.4 %multiply_convert_fusion = bf16[512,3072]{1,0:T(8,128)(2,1)} fusion(bf16[512,1536]{1,0:T(8,128)(2,1)S(1)} %attention.1, bf16[1536,3072]{1,0:T(8,128)(2,1)S(1)} %copy-done.1, f32[3072]{0:T(1024)S(1)} %copy-done.2), kind=kOutput, calls=%fused_computation | convolution fusion | flops 4834983936 | bytes 14168064 | tf_op jit(solution)/shard_map/dot_general | solution.py:557
Async XLA Ops:
  0.8 0.8 copy-start
  1.6 153.4 %copy-start.1 = (bf16[1536,3072]{1,0:T(8,128)(2,1)S(1)}, bf16[1536,3072]{1,0:T(8,128)(2,1)}, u32[]{:S(2)}) copy-start(bf16[1536,3072]{1,0:T(8,128)(2,1)} %param.15) | copy-start | bytes 28311556
  1.6 153.4 %copy-start.2 = (f32[3072]{0:T(1024)S(1)}, f32[3072]{0:T(1024)}, u32[]{:S(2)}) copy-start(f32[3072]{0:T(1024)} %param.16) | copy-start | bytes 36868

commit v5 on v3

--- a/solution.py
+++ b/solution.py
@@ -26,7 +26,7 @@
 N_MAIN = SLOTS - MAIN
 MID = COLS // 2
 GROUPS = ((0, 48), (48, 32), (80, 32), (112, 16))
-EARLY = 4
+EARLY, BRIDGE = 4, 14
 
 
 def blend(late, before, after):
@@ -424,6 +424,11 @@
                    halves=(None,), last=group == len(GROUPS) - 1)
 
     use_far(0)
+
+    @pl.loop(EARLY, BRIDGE)
+    def _(p):
+        send_main(p)
+
     wait_halo(NORTH)
     wait_halo(SOUTH)
     for i, piece in enumerate((NW, NE, SW, SE)):
@@ -433,7 +438,7 @@
                 pack(ref, 0, R, piece in (NW, SW), corner_ref.at[2 * i + n])
         start_halo(piece)
 
-    @pl.loop(EARLY, N_MAIN)
+    @pl.loop(BRIDGE, N_MAIN)
     def _(p):
         send_main(p)
 

time: 158 us -> 158 us (level)
  no operation moved by 1% of the time
where the time goes in v5:
time: 158 us
  Pallas kernels  150 us (95%)
  matrix products  6.4 us (4%)
    pallas_call x1, Pallas kernels, shards(): pl.pallas_call(kernel, out_shape=jax.ShapeDtypeStruct((tokens, inner), bf...  150 us
    dot_general x1, matrix products, shards(): jnp.dot(attended, weight_out, preferred_element_type=jnp.float32)  6.4 us

profile of v5, /device:TPU:1, one launch (start us, length us, event | category | flops | bytes accessed | tf_op | source)
XLA Modules:
  0.0 157.7 jit_solution(11214183133522927830)
XLA Ops:
  0.0 0.8 select_reduce_fusion.block_of
  0.8 0.0 copy-start
  0.8 0.8 copy-done
  1.6 0.0 copy-start.1
  1.6 0.0 copy-start.2
  1.6 149.6 %attention.1 = bf16[512,1536]{1,0:T(8,128)(2,1)S(1)} custom-call(bf16[512,1536]{1,0:T(8,128)(2,1)} %bitcast.8, bf16[16,32,1536]{2,1,0:T(8,128)(2,1)} %k_hbm.1, bf16[16,32,1536]{2,1,0:T(8,128)(2,1)} %v_hbm.1, bf16[32,16,1536]{2,1,0:T(8,128)(2,1)} %bitcast.9, bf16[32,16,1536]{2,1,0:T(8,128)(2,1)} %bitcast.10, s32[80,128]{1,0:T(8,128)S(1)} %bitcast.7, ...), custom_call_target="tpu_custom_call" | custom-call | tf_op jit(solution)/shard_map/attention/pallas_call | solution.py:513
  151.2 0.0 copy-done.1
  151.3 0.0 copy-done.2
  151.3 6.4 %multiply_convert_fusion = bf16[512,3072]{1,0:T(8,128)(2,1)} fusion(bf16[512,1536]{1,0:T(8,128)(2,1)S(1)} %attention.1, bf16[1536,3072]{1,0:T(8,128)(2,1)S(1)} %copy-done.1, f32[3072]{0:T(1024)S(1)} %copy-done.2), kind=kOutput, calls=%fused_computation | convolution fusion | flops 4834983936 | bytes 14168064 | tf_op jit(solution)/shard_map/dot_general | solution.py:560
Async XLA Ops:
  0.8 0.8 copy-start
  1.6 149.6 %copy-start.1 = (bf16[1536,3072]{1,0:T(8,128)(2,1)S(1)}, bf16[1536,3072]{1,0:T(8,128)(2,1)}, u32[]{:S(2)}) copy-start(bf16[1536,3072]{1,0:T(8,128)(2,1)} %param.15) | copy-start | bytes 28311556
  1.6 149.6 %copy-start.2 = (f32[3072]{0:T(1024)S(1)}, f32[3072]{0:T(1024)}, u32[]{:S(2)}) copy-start(f32[3072]{0:T(1024)} %param.16) | copy-start | bytes 36868
